TPU v7x, 32 devices: a whole 2x2x4 slice. The times are simulated.
32 devices in a mesh: tile: 4 (over z), train: 8 (over y, x, core).
Axes of the slice: x: 2, y: 2, z: 4, core: 2. Of those that a mesh axis runs over, the one named last changes fastest.
Arguments:
- columns: bfloat16 [32768, 512], P(('tile', 'train')), may hold values from -6 to 6
- truth: bfloat16 [32768, 128], P(('tile', 'train')), may hold values from -6 to 6
- weight_in: bfloat16 [512, 1024], replicated, may hold values from -0.25 to 0.25
- weight_out: bfloat16 [1024, 128], replicated, may hold values from -0.1875 to 0.1875
- master_in: float32 [512, 1024], P(None, 'tile'), may hold values from -0.25 to 0.25
- master_out: float32 [1024, 128], P('tile'), may hold values from -0.1875 to 0.1875
- moment_in: float32 [512, 1024], P(None, 'tile'), may hold values from -6 to 6
- moment_out: float32 [1024, 128], P('tile'), may hold values from -6 to 6
- second_in: float32 [512, 1024], P(None, 'tile'), may hold values from 1 to 30
- second_out: float32 [1024, 128], P('tile'), may hold values from 1 to 30
- counts: int32 [32], P(('tile', 'train')), may hold values from 1 to 16, as said below
- sampled: int32 [512, 128], P(('tile', 'train')), may hold values from 0 to 1023
- routes: int32 [512, 1], P(('tile', 'train')), may hold values from 0 to 7; in each aligned block of 16 rows (0 to 15, 16 to 31, ...) at most 2 rows name the same one
Outputs:
- predicted: bfloat16 [32768, 128], P(('tile', 'train'))
- trainer_loss: float32 [32], P(('tile', 'train'))
- fresh_in: bfloat16 [512, 1024], replicated
- fresh_out: bfloat16 [1024, 128], replicated
- new_master_in: float32 [512, 1024], P(None, 'tile')
- new_master_out: float32 [1024, 128], P('tile')
- new_moment_in: float32 [512, 1024], P(None, 'tile')
- new_moment_out: float32 [1024, 128], P('tile')
- new_second_in: float32 [512, 1024], P(None, 'tile')
- new_second_out: float32 [1024, 128], P('tile')
Inputs may be any that keep to these rules, and one draw needn't show every extreme that they name: `counts`: one device's count reaches 16; the others are at most 10. `routes`: among the 16 slots of one device every trainer is named by exactly 2 slots.
All inputs are finite; a program needn't handle non-finite values.
Results may differ from a plain program's by a relative error of at most 0.0049.
Values may be sent and summed in bfloat16 or wider, within the bound.
A program may use at most 64 MiB of HBM per device.

v0:
```python
import jax
import jax.numpy as jnp
from jax import lax
from jax.sharding import PartitionSpec as P

BLK = 128


rate = 0.001
first_fix = 1.0 - 0.9**8
second_fix = 1.0 - 0.999**8


def silu_slope(pre):
    sig = jax.nn.sigmoid(pre)
    return sig * (1.0 + pre * (1.0 - sig))


def adam_update(master, moment, second, grad):
    moment = 0.9 * moment + 0.1 * grad
    second = 0.999 * second + 0.001 * grad * grad
    master = master - rate * (moment / first_fix) / (jnp.sqrt(second / second_fix) + 1e-08)
    return (master, moment, second)


def local(
    columns,
    truth,
    weight_in,
    weight_out,
    master_in,
    master_out,
    moment_in,
    moment_out,
    second_in,
    second_out,
    counts,
    sampled,
    routes,
):
    f32 = jnp.float32
    trainers = lax.axis_size("train")
    live = jnp.arange(sampled.shape[0], dtype=jnp.int32) < counts[0]
    named = routes == jnp.arange(trainers, dtype=jnp.int32)[None, :]
    kinds = jnp.concatenate([named & live[:, None], live[:, None]], axis=1)
    hit = sampled.reshape(1, -1) == jnp.arange(columns.shape[0], dtype=jnp.int32)[:, None]
    times = jnp.dot(
        hit.astype(jnp.bfloat16),
        jnp.repeat(kinds, BLK, axis=0).astype(jnp.bfloat16),
        preferred_element_type=f32,
    )
    pre = jnp.dot(columns, weight_in, preferred_element_type=f32)
    hidden = jax.nn.silu(pre).astype(jnp.bfloat16)
    output = jnp.dot(hidden, weight_out, preferred_element_type=f32)
    predicted = output.astype(jnp.bfloat16)
    error = output - truth.astype(f32)
    squares = jnp.sum(error * error, axis=1, keepdims=True)
    losses = lax.psum(jnp.sum(squares * times[:, :trainers], axis=0), "train")
    me = lax.axis_index("train")
    trainer_loss = lax.dynamic_slice_in_dim(losses, me, 1) / (BLK * weight_out.shape[1])
    often = times[:, trainers:]
    hidden_grad = jnp.dot(error.astype(jnp.bfloat16), weight_out.T, preferred_element_type=f32)
    pre_grad = (often * hidden_grad * silu_slope(pre)).astype(jnp.bfloat16)
    grad_in = jnp.dot(columns.T, pre_grad, preferred_element_type=f32)
    grad_out = jnp.dot(hidden.T, (often * error).astype(jnp.bfloat16), preferred_element_type=f32)
    scale = 2.0 / BLK
    share_in = lax.psum_scatter(grad_in, "tile", scatter_dimension=1, tiled=True)
    share_out = lax.psum_scatter(grad_out, "tile", scatter_dimension=0, tiled=True)
    share_in, share_out = lax.psum((share_in, share_out), "train")
    new_master_in, new_moment_in, new_second_in = adam_update(
        master_in, moment_in, second_in, scale * share_in
    )
    new_master_out, new_moment_out, new_second_out = adam_update(
        master_out, moment_out, second_out, scale * share_out
    )
    rounded_in = new_master_in.astype(jnp.bfloat16)
    rounded_out = new_master_out.astype(jnp.bfloat16)
    fresh_in, fresh_out = (
        lax.all_gather(rounded_in, "tile", axis=1, tiled=True),
        lax.all_gather(rounded_out, "tile", axis=0, tiled=True),
    )
    return (
        predicted,
        trainer_loss,
        fresh_in,
        fresh_out,
        new_master_in,
        new_master_out,
        new_moment_in,
        new_moment_out,
        new_second_in,
        new_second_out,
    )


def solution(mesh):
    return jax.shard_map(
        local,
        mesh=mesh,
        in_specs=(
            P(("tile", "train"), None),
            P(("tile", "train"), None),
            P(),
            P(),
            P(None, "tile"),
            P("tile", None),
            P(None, "tile"),
            P("tile", None),
            P(None, "tile"),
            P("tile", None),
            P(("tile", "train")),
            P(("tile", "train"), None),
            P(("tile", "train"), None),
        ),
        out_specs=(
            P(("tile", "train"), None),
            P(("tile", "train")),
            P(),
            P(),
            P(None, "tile"),
            P("tile", None),
            P(None, "tile"),
            P("tile", None),
            P(None, "tile"),
            P("tile", None),
        ),
        check_vma=False,
    )
```

profile of v0, /device:TPU:0, one launch (start us, length us, event | category | flops | bytes accessed | tf_op | source)
XLA Modules:
  0.0 194.2 jit_solution(5880691147949128025)
XLA Ops:
  7.2 1.2 copy.23
  9.2 0.7 fusion.7
  10.0 2.3 %fusion = f32[1024,9]{0,1:T(8,128)S(1)} fusion(pred[2048,9]{1,0:T(32,128)(4,1)S(1)} %bitcast.17, s32[2048]{0:T(1024)} %bitcast.21), kind=kOutput, calls=%fused_computation.1 | convolution fusion | flops 39845888 | bytes 63488 | tf_op jit(solution)/shard_map/dot_general | solution.py:47
  12.3 0.6 copy-done.5
  13.0 3.5 %multiply_convert_fusion.1 = (bf16[1024,1024]{1,0:T(8,128)(2,1)S(1)}, f32[1024,1024]{1,0:T(8,128)}) fusion(bf16[1024,512]{1,0:T(8,128)(2,1)S(1)} %copy-done, bf16[512,1024]{1,0:T(8,128)(2,1)S(1)} %copy-done.6), kind=kOutput, calls=%fused_computation.4 | convolution fusion | flops 1078984704 | bytes 8388608 | tf_op jit(solution)/shard_map/dot_general | solution.py:52
  16.5 0.8 multiply_reduce_fusion
  17.3 1.6 fusion.2
  19.0 5.9 %convolution_bitcast_fusion = f32[512,1024]{0,1:T(8,128)} fusion(bf16[1024,512]{1,0:T(8,128)(2,1)S(1)} %copy-done, f32[1024,1024]{1,0:T(8,128)} %get-tuple-element.33, bf16[1024,128]{1,0:T(8,128)(2,1)S(1)} %copy-done.3, f32[1024]{0:T(1024)S(1)} %bitcast.19, f32[1024,128]{0,1:T(8,128)S(1)} %get-tuple-element.34, bf16[1024,128]{0,1:T(8,128)(2,1)S(1)} %copy.23), kind=kOutput, calls=%fused_computation.6 | convolution fusion | flops 1353056256 | bytes 8392704 | tf_op jit(solution)/shard_map/dot_general | solution.py:64
  25.0 18.4 %reduce-scatter.5.cloned.1.call-done = f32[256,128]{1,0:T(8,128)} async-done(((f32[1024,128]{1,0:T(8,128)}), f32[256,128]{1,0:T(8,128)}) %reduce-scatter.5.cloned.1.call-update) | async-done | bytes 131088 | tf_op jit(solution)/shard_map/reduce_scatter | solution.py:68
  43.4 44.5 %reduce-scatter.3.cloned.1.call-done = f32[512,256]{0,1:T(8,128)} async-done(((f32[512,1024]{0,1:T(8,128)}), f32[512,256]{0,1:T(8,128)}) %reduce-scatter.3.cloned.1.call-update) | async-done | bytes 524304 | tf_op jit(solution)/shard_map/reduce_scatter | solution.py:67
  88.2 2.0 %copy.25 = f32[512,256]{0,1:T(8,128)} copy(f32[512,256]{1,0:T(8,128)} %param.21) | data formatting | bytes 1048576 | tf_op args[8]
  90.3 1.0 copy.26
  91.2 54.7 %all-reduce.3.cloned.1.call-done = (f32[512,256]{0,1:T(8,128)}, f32[256,128]{1,0:T(8,128)}) async-done(((f32[512,256]{0,1:T(8,128)}, f32[256,128]{1,0:T(8,128)}), (f32[512,256]{0,1:T(8,128)}, f32[256,128]{1,0:T(8,128)})) %all-reduce.3.cloned.1.call-update) | async-done | bytes 655376 | tf_op jit(solution)/shard_map/psum | solution.py:69
  146.0 2.4 %fusion.10 = (bf16[512,256]{0,1:T(8,128)(2,1)}, f32[512,256]{0,1:T(8,128)S(1)}, f32[512,256]{0,1:T(8,128)S(1)}, f32[512,256]{0,1:T(8,128)S(1)}) fusion(f32[512,256]{0,1:T(8,128)} %copy.26, f32[512,256]{0,1:T(8,128)} %get-tuple-element.20, f32[512,256]{0,1:T(8,128)S(1)} %copy.24, f32[512,256]{0,1:T(8,128)} %copy.25), kind=kLoop, calls=%fused_computation.28 | loop fusion | flops 1835008 | bytes 3932160 | tf_op jit(solution)/shard_map/convert_element_type | solution.py:76
  148.4 0.9 fusion.6
  149.3 11.8 %psum.21 = f32[8]{0:T(128)S(1)} all-reduce(f32[8]{0:T(128)S(1)} %fusion.6), channel_id=1, replica_groups=mesh['tile'=4,'train'=8] {'train'}, use_global_device_ids=true, to_apply=%region_2.3 | all-reduce | flops 8 | bytes 64 | tf_op jit(solution)/shard_map/psum | solution.py:58
  161.1 0.8 copy.27
  163.2 1.0 copy.29
  164.2 1.0 copy.30
  165.2 1.0 copy.31
  166.2 1.8 fusion.9
  168.0 15.6 %all_gather.7 = bf16[1024,128]{1,0:T(8,128)(2,1)S(1)} all-gather(bf16[256,128]{1,0:T(8,128)(2,1)S(1)} %get-tuple-element.22), channel_id=1, replica_groups=mesh['tile'=4,'train'=8] {'tile'}, dimensions={0}, use_global_device_ids=true | all-gather | bytes 327680 | tf_op jit(solution)/shard_map/all_gather | solution.py:80
  183.5 2.3 %copy.28 = bf16[512,1024]{1,0:T(8,128)(2,1)} copy(bf16[512,1024]{0,1:T(8,128)(2,1)} %all-gather.2.cloned.1.call-done) | data formatting | bytes 2097152
  185.8 0.7 copy.37
  (29 shorter events, 1.2 us)
Async XLA Ops:
  7.2 5.8 %copy-start = (bf16[1024,512]{1,0:T(8,128)(2,1)S(1)}, bf16[1024,512]{1,0:T(8,128)(2,1)}, u32[]{:S(2)}) copy-start(bf16[1024,512]{1,0:T(8,128)(2,1)} %param.13) | copy-start | bytes 3145732
  7.2 5.8 %copy-start.6 = (bf16[512,1024]{1,0:T(8,128)(2,1)S(1)}, bf16[512,1024]{1,0:T(8,128)(2,1)}, u32[]{:S(2)}) copy-start(bf16[512,1024]{1,0:T(8,128)(2,1)} %param.15) | copy-start | bytes 3145732
  7.2 36.2 %reduce-scatter.5.cloned.1.call-start = ((), (), s32[]{:S(2)}) async-start(), calls=%async_computation.4 | async-start | bytes 655360 | tf_op jit(solution)/shard_map/reduce_scatter | solution.py:68
  12.3 0.6 copy-start.5
  13.0 3.5 %copy-start.3 = (bf16[1024,128]{1,0:T(8,128)(2,1)S(1)}, bf16[1024,128]{1,0:T(8,128)(2,1)}, u32[]{:S(2)}) copy-start(bf16[1024,128]{1,0:T(8,128)(2,1)} %param.16) | copy-start | bytes 786436
  18.9 69.0 %reduce-scatter.3.cloned.1.call-start = ((), (), s32[]{:S(2)}) async-start(), calls=%async_computation.2 | async-start | bytes 2621440 | tf_op jit(solution)/shard_map/reduce_scatter | solution.py:67
  19.0 69.0 %copy-start.1 = (f32[512,256]{1,0:T(8,128)S(1)}, f32[512,256]{1,0:T(8,128)}, u32[]{:S(2)}) copy-start(f32[512,256]{1,0:T(8,128)} %param.19) | copy-start | bytes 1572868
  24.9 65.3 %copy-start.2 = (f32[512,256]{1,0:T(8,128)S(1)}, f32[512,256]{1,0:T(8,128)}, u32[]{:S(2)}) copy-start(f32[512,256]{1,0:T(8,128)} %param.17) | copy-start | bytes 1572868
  25.0 121.0 %all-reduce.3.cloned.1.call-start = ((), (), s32[]{:S(2)}) async-start(), calls=%async_computation.5 | async-start | bytes 1310720 | tf_op jit(solution)/shard_map/psum | solution.py:69
  87.9 95.6 %all-gather.2.cloned.1.call-start = ((), (), s32[]{:S(2)}) async-start(), calls=%async_computation.3 | async-start | bytes 1310720 | tf_op jit(solution)/shard_map/all_gather | solution.py:79
  91.2 74.9 %copy-start.4 = (f32[256,128]{1,0:T(8,128)S(1)}, f32[256,128]{1,0:T(8,128)}, u32[]{:S(2)}) copy-start(f32[256,128]{1,0:T(8,128)} %param.18) | copy-start | bytes 393220
Sparse Core Ops, SparseCore 0:
  19.1 24.3 reduce-scatter.4
  45.7 42.1 reduce-scatter.2
  91.4 54.4 all-reduce.2
  148.5 29.8 all-gather.1
where the time goes:
time: 195 us; the launch traced here: 194 us
  waiting for transfers between devices  118 us (61%)
  blocking collectives  27.3 us (14%)
  between operations  16.3 us (8%)
  matrix products  14.1 us (7%)
  local copies, waits for them, and re-layouts  12.6 us (6%)
  other arithmetic  5.97 us (3%)
    psum x1, waiting for transfers between devices, local(): share_in, share_out = lax.psum((share_in, share_out), 'train')  54.7 us
    reduce_scatter x1, waiting for transfers between devices, local(): lax.psum_scatter(grad_in, 'tile', scatter_dimension=1, tiled=True)  44.5 us
    reduce_scatter x1, waiting for transfers between devices, local(): lax.psum_scatter(grad_out, 'tile', scatter_dimension=0, tiled=True)  18.4 us
    all_gather x1, blocking collectives, local(): lax.all_gather(rounded_out, 'tile', axis=0, tiled=True)  15.6 us
    unnamed x24, local copies, waits for them, and re-layouts  11.9 us
    psum x1, blocking collectives, local(): losses = lax.psum(jnp.sum(squares * times[:, :trainers], axis=0), 'train')  11.8 us
    dot_general x1, matrix products, local(): grad_in = jnp.dot(columns.T, pre_grad, preferred_element_type=f32)  5.94 us
  transfers between devices with their start and end apart: 4, of which 3 were waited for; matrix products, arithmetic and copies ran while one was open for 8% of the time, Pallas kernels for 0%

commit v1 on v0

v1 whole, which is shorter than its diff:
```python
import functools
import jax
import jax.numpy as jnp
from jax import lax
from jax.experimental import pallas as pl
from jax.experimental.pallas import tpu as pltpu
from jax.sharding import PartitionSpec as P

BLK = 128
LANES = 128
STREAMS = 2
CHUNK = 256

rate = 0.001
first_fix = 1.0 - 0.9**8
second_fix = 1.0 - 0.999**8
f32, bf16 = jnp.float32, jnp.bfloat16


def adam_update(master, moment, second, grad):
    moment = 0.9 * moment + 0.1 * grad
    second = 0.999 * second + 0.001 * grad * grad
    master = master - rate * (moment / first_fix) / (jnp.sqrt(second / second_fix) + 1e-08)
    return (master, moment, second)


def bits_of(size):
    return size.bit_length() - 1


def stream_orders(trainers):
    ascending = list(range(bits_of(trainers)))
    return [ascending, ascending[:1] + ascending[:0:-1]]


def place_of(index, order):
    place = 0
    for bit in order:
        place = place * 2 + (index // 2**bit) % 2
    return place


def kernel(
    tiles, trainers,
    columns, truth, weight_in, weight_out,
    master_in, master_out, moment_in, moment_out, second_in, second_out,
    counts, sampled, routes,
    predicted, trainer_loss, fresh_in, fresh_out,
    new_master_in, new_master_out, new_moment_in, new_moment_out, new_second_in, new_second_out,
    marks, pre_grads, hiddens, backs, loss_rows,
    total, outgoing, arrived_train, arrived_tile, gathered, fresh, loss_out, loss_in,
    send_sem, recv_sem,
):
    t, u = lax.axis_index("tile"), lax.axis_index("train")
    train_bits, tile_bits = bits_of(trainers), bits_of(tiles)
    orders = stream_orders(trainers)
    tile_order = list(range(tile_bits))
    piece = total.shape[3]
    share_rows = STREAMS * trainers * piece
    feat, width = master_in.shape
    height = master_out.shape[0]
    blocks_in = width // LANES

    def bit_of(axis, bit):
        return ((u if axis == "train" else t) // 2**bit) % 2

    def partner(axis, bit):
        index = u if axis == "train" else t
        return {axis: index + 2**bit * (1 - 2 * bit_of(axis, bit))}

    barrier = pltpu.get_barrier_semaphore()
    for axis, number in (("train", train_bits), ("tile", tile_bits)):
        for bit in range(number):
            pl.semaphore_signal(
                barrier, inc=1, device_id=partner(axis, bit), device_id_type=pl.DeviceIdType.MESH
            )

    slots = sampled.shape[0]
    lane = lax.broadcasted_iota(jnp.int32, (slots, LANES), 1)
    slot = lax.broadcasted_iota(jnp.int32, (slots, LANES), 0)
    named = (lane >= trainers) | (routes[...] == lane)
    kinds = jnp.where(named & (slot < counts[...]), 1.0, 0.0).astype(f32)
    for b in range(slots):
        marks[b * BLK : (b + 1) * BLK, :] = jnp.broadcast_to(
            kinds[b : b + 1, :], (BLK, LANES)
        ).astype(bf16)
    loss_rows[...] = jnp.zeros_like(loss_rows)

    def chunk(step, carry):
        start = pl.multiple_of(step * CHUNK, CHUNK)
        rows = pl.ds(start, CHUNK)
        own = lax.broadcasted_iota(jnp.int32, (CHUNK, LANES), 0) + start
        hits = jnp.concatenate(
            [jnp.where(own == sampled[b : b + 1, :], 1.0, 0.0).astype(bf16) for b in range(slots)],
            axis=1,
        )
        times = jnp.dot(hits, marks[...], preferred_element_type=f32)
        pre = jnp.dot(columns[rows, :], weight_in[...], preferred_element_type=f32)
        sig = 0.5 + 0.5 * jnp.tanh(0.5 * pre)
        value = pre * sig
        hidden = value.astype(bf16)
        hiddens[rows, :] = hidden
        output = jnp.dot(hidden, weight_out[...], preferred_element_type=f32)
        predicted[rows, :] = output.astype(bf16)
        error = output - truth[rows, :].astype(f32)
        squares = jnp.sum(error * error, axis=1, keepdims=True)
        loss_rows[...] += jnp.sum((squares * times).reshape(CHUNK // 8, 8, LANES), axis=0)
        often = times[:, LANES - 1 :]
        backs[rows, :] = (often * error).astype(bf16)
        hidden_grad = lax.dot_general(
            error.astype(bf16), weight_out[...], (((1,), (1,)), ((), ())),
            preferred_element_type=f32,
        )
        pre_grads[rows, :] = (often * hidden_grad * (sig + value * (1.0 - sig))).astype(bf16)
        return carry

    lax.fori_loop(0, columns.shape[0] // CHUNK, chunk, 0)

    for tile in range(tiles):
        place = place_of(tile, tile_order)
        across = slice(tile * width, (tile + 1) * width)
        part_in = lax.dot_general(
            columns[...], pre_grads[:, across], (((0,), (0,)), ((), ())),
            preferred_element_type=f32,
        )
        part_out = lax.dot_general(
            hiddens[:, tile * height : (tile + 1) * height], backs[...], (((0,), (0,)), ((), ())),
            preferred_element_type=f32,
        )
        parts = [part_in[:, c * LANES : (c + 1) * LANES] for c in range(blocks_in)] + [part_out]
        missing = share_rows - blocks_in * feat - height
        if missing:
            parts.append(jnp.zeros((missing, LANES), f32))
        total[:, :, place] = jnp.concatenate(parts, axis=0).reshape(
            STREAMS, trainers, piece, LANES
        )

    pl.semaphore_wait(barrier, train_bits + tile_bits)

    used = [0]
    pending = []

    def send(source, target, axis, bit):
        number = used[0]
        used[0] += 1
        copy = pltpu.make_async_remote_copy(
            src_ref=source,
            dst_ref=target,
            send_sem=send_sem.at[number],
            recv_sem=recv_sem.at[number],
            device_id=partner(axis, bit),
            device_id_type=pl.DeviceIdType.MESH,
        )
        copy.start()
        pending.append(copy)
        return copy

    starts = [0] * STREAMS
    flying = [None] * STREAMS
    losses = loss_rows[...]
    loss_copy = None
    for step in range(train_bits):
        half = 2 ** (train_bits - 1 - step)
        if loss_copy is not None:
            loss_copy.wait_recv()
            losses = losses + loss_in[step - 1]
        loss_out[step] = losses
        loss_copy = send(loss_out.at[step], loss_in.at[step], "train", step)
        for s in range(STREAMS):
            if step:
                flying[s].wait_recv()
                total[s, pl.ds(starts[s], 2 * half)] += arrived_train[s, 2 * half : 4 * half].astype(f32)
            bit = orders[s][step]
            mine = bit_of("train", bit)
            away = pl.ds(starts[s] + (1 - mine) * half, half)
            outgoing[s, away] = total[s, away].astype(bf16)
            flying[s] = send(
                outgoing.at[s, away], arrived_train.at[s, pl.ds(half, half)], "train", bit
            )
            starts[s] = starts[s] + mine * half
    loss_copy.wait_recv()
    losses = losses + loss_in[train_bits - 1]
    mine_only = lax.broadcasted_iota(jnp.int32, losses.shape, 1) == u
    trainer_loss[...] = jnp.sum(
        jnp.where(mine_only, losses, 0.0), axis=(0, 1), keepdims=True
    ) / (BLK * weight_out.shape[1])

    spots = [0] * STREAMS
    for step in range(tile_bits):
        half = 2 ** (tile_bits - 1 - step)
        for s in range(STREAMS):
            flying[s].wait_recv()
            if step == 0:
                total[s, starts[s]] += arrived_train[s, 1].astype(f32)
            else:
                total[s, starts[s], pl.ds(spots[s], 2 * half)] += arrived_tile[
                    s, 2 * half : 4 * half
                ].astype(f32)
            bit = tile_order[step]
            mine = bit_of("tile", bit)
            away = pl.ds(spots[s] + (1 - mine) * half, half)
            outgoing[s, starts[s], away] = total[s, starts[s], away].astype(bf16)
            flying[s] = send(
                outgoing.at[s, starts[s], away], arrived_tile.at[s, pl.ds(half, half)], "tile", bit
            )
            spots[s] = spots[s] + mine * half

    begin = [None] * STREAMS
    for s in range(STREAMS):
        flying[s].wait_recv()
        done = total[s, starts[s], spots[s]] + arrived_tile[s, 1].astype(f32)
        gathered[s, starts[s]] = done.astype(bf16)
        begin[s] = starts[s]
    for step in reversed(range(train_bits)):
        size = 2 ** (train_bits - 1 - step)
        for s in range(STREAMS):
            if step < train_bits - 1:
                flying[s].wait_recv()
                begin[s] = begin[s] - bit_of("train", orders[s][step + 1]) * (size // 2)
            region = gathered.at[s, pl.ds(begin[s], size)]
            flying[s] = send(region, region, "train", orders[s][step])
    for s in range(STREAMS):
        flying[s].wait_recv()

    grads = gathered[...].reshape(share_rows, LANES)
    scale = 2.0 / BLK
    shares = []
    for c in range(blocks_in):
        across = slice(c * LANES, (c + 1) * LANES)
        grad = scale * grads[c * feat : (c + 1) * feat].astype(f32)
        master, moment, second = adam_update(
            master_in[:, across], moment_in[:, across], second_in[:, across], grad
        )
        new_master_in[:, across] = master
        new_moment_in[:, across] = moment
        new_second_in[:, across] = second
        shares.append(master.astype(bf16))
    grad = scale * grads[blocks_in * feat : blocks_in * feat + height].astype(f32)
    master, moment, second = adam_update(master_out[...], moment_out[...], second_out[...], grad)
    new_master_out[...] = master
    new_moment_out[...] = moment
    new_second_out[...] = second
    shares.append(master.astype(bf16))
    missing = share_rows - blocks_in * feat - height
    if missing:
        shares.append(jnp.zeros((missing, LANES), bf16))
    for copy in pending:
        copy.wait_send()
    pending.clear()
    gathered[...] = jnp.concatenate(shares, axis=0).reshape(gathered.shape)
    for s in range(STREAMS):
        fresh[s, starts[s], spots[s]] = gathered[s, starts[s]]
    begin = list(spots)
    for step in reversed(range(tile_bits)):
        size = 2 ** (tile_bits - 1 - step)
        for s in range(STREAMS):
            if step < tile_bits - 1:
                flying[s].wait_recv()
                begin[s] = begin[s] - bit_of("tile", tile_order[step + 1]) * (size // 2)
            region = fresh.at[s, starts[s], pl.ds(begin[s], size)]
            flying[s] = send(region, region, "tile", tile_order[step])
    begin = list(starts)
    for step in reversed(range(train_bits)):
        size = 2 ** (train_bits - 1 - step)
        for s in range(STREAMS):
            flying[s].wait_recv()
            if step < train_bits - 1:
                begin[s] = begin[s] - bit_of("train", orders[s][step + 1]) * (size // 2)
            region = fresh.at[s, pl.ds(begin[s], size)]
            flying[s] = send(region, region, "train", orders[s][step])
    for s in range(STREAMS):
        flying[s].wait_recv()
    for tile in range(tiles):
        flat = fresh[:, :, place_of(tile, tile_order)].reshape(share_rows, LANES)
        for c in range(blocks_in):
            left = tile * width + c * LANES
            fresh_in[:, left : left + LANES] = flat[c * feat : (c + 1) * feat]
        fresh_out[tile * height : (tile + 1) * height, :] = flat[
            blocks_in * feat : blocks_in * feat + height
        ]
    for copy in pending:
        copy.wait_send()


def local(
    columns, truth, weight_in, weight_out,
    master_in, master_out, moment_in, moment_out, second_in, second_out,
    counts, sampled, routes,
):
    tiles, trainers = lax.axis_size("tile"), lax.axis_size("train")
    train_bits, tile_bits = bits_of(trainers), bits_of(tiles)
    rows, feat = columns.shape
    hidden, outs = weight_out.shape
    slots = sampled.shape[0]
    needed = (feat * master_in.shape[1] + master_out.shape[0] * outs) // LANES
    piece = -(-needed // (STREAMS * trainers * 16)) * 16
    copies = (2 * STREAMS) * (train_bits + tile_bits) + STREAMS * train_bits + train_bits
    like = lambda a: jax.ShapeDtypeStruct(a.shape, a.dtype)
    results = pl.pallas_call(
        functools.partial(kernel, tiles, trainers),
        out_shape=(
            like(truth),
            jax.ShapeDtypeStruct((1, 1), f32),
            like(weight_in),
            like(weight_out),
            like(master_in), like(master_out),
            like(moment_in), like(moment_out),
            like(second_in), like(second_out),
        ),
        in_specs=[pl.BlockSpec(memory_space=pltpu.VMEM)] * 13,
        out_specs=(pl.BlockSpec(memory_space=pltpu.VMEM),) * 10,
        scratch_shapes=[
            pltpu.VMEM((slots * BLK, LANES), bf16),
            pltpu.VMEM((rows, hidden), bf16),
            pltpu.VMEM((rows, hidden), bf16),
            pltpu.VMEM((rows, outs), bf16),
            pltpu.VMEM((8, LANES), f32),
            pltpu.VMEM((STREAMS, trainers, tiles, piece, LANES), f32),
            pltpu.VMEM((STREAMS, trainers, tiles, piece, LANES), bf16),
            pltpu.VMEM((STREAMS, trainers, tiles, piece, LANES), bf16),
            pltpu.VMEM((STREAMS, tiles, piece, LANES), bf16),
            pltpu.VMEM((STREAMS, trainers, piece, LANES), bf16),
            pltpu.VMEM((STREAMS, trainers, tiles, piece, LANES), bf16),
            pltpu.VMEM((train_bits, 8, LANES), f32),
            pltpu.VMEM((train_bits, 8, LANES), f32),
            pltpu.SemaphoreType.DMA((copies,)),
            pltpu.SemaphoreType.DMA((copies,)),
        ],
        compiler_params=pltpu.CompilerParams(
            collective_id=0, has_side_effects=True, vmem_limit_bytes=48 * 2**20
        ),
    )(
        columns, truth, weight_in, weight_out,
        master_in, master_out, moment_in, moment_out, second_in, second_out,
        counts.reshape(1, 1), sampled, routes,
    )
    return (results[0], results[1].reshape(1)) + tuple(results[2:])


def solution(mesh):
    return jax.shard_map(
        local,
        mesh=mesh,
        in_specs=(
            P(("tile", "train"), None),
            P(("tile", "train"), None),
            P(),
            P(),
            P(None, "tile"),
            P("tile", None),
            P(None, "tile"),
            P("tile", None),
            P(None, "tile"),
            P("tile", None),
            P(("tile", "train")),
            P(("tile", "train"), None),
            P(("tile", "train"), None),
        ),
        out_specs=(
            P(("tile", "train"), None),
            P(("tile", "train")),
            P(),
            P(),
            P(None, "tile"),
            P("tile", None),
            P(None, "tile"),
            P("tile", None),
            P(None, "tile"),
            P("tile", None),
        ),
        check_vma=False,
    )
```

time: 195 us -> 72 us (0.37)
  waiting for transfers between devices: 118 us -> 0 us
  Pallas kernels: 0 us -> 53 us
  blocking collectives: 27.3 us -> 0 us
  matrix products: 14.1 us -> 0 us
  between operations: 16.3 us -> 3.09 us
  other arithmetic: 5.97 us -> 0 us
  local copies, waits for them, and re-layouts: 12.6 us -> 15.2 us
    reduce_scatter x2 -> x0, waiting for transfers between devices: 62.9 us -> none  [the longest x1 44.5 us: local(): lax.psum_scatter(grad_in, 'tile', scatter_dimension=1, tiled=True)]
    psum x1 -> x0, waiting for transfers between devices: 54.7 us -> none  [local(): share_in, share_out = lax.psum((share_in, share_out), 'train')]
    pallas_call x0 -> x1, Pallas kernels: none -> 53 us  [local(): pl.pallas_call(functools.partial(kernel, tiles, trainers), out_shape=(lik...]
    all_gather x1 -> x0, blocking collectives: 15.6 us -> none  [local(): lax.all_gather(rounded_out, 'tile', axis=0, tiled=True)]
    dot_general x5 -> x0, matrix products: 14.1 us -> none  [the longest x1 5.94 us: local(): grad_in = jnp.dot(columns.T, pre_grad, preferred_element_type=f32)]
    psum x1 -> x0, blocking collectives: 11.8 us -> none  [local(): losses = lax.psum(jnp.sum(squares * times[:, :trainers], axis=0), 'train')]
    convert_element_type x2 -> x0, other arithmetic: 4.27 us -> none  [the longest x1 2.45 us: local(): rounded_in = new_master_in.astype(jnp.bfloat16)]
    unnamed x24 -> x28, local copies, waits for them, and re-layouts: 11.9 us -> 15.2 us
  transfers between devices with their start and end apart: 4 -> 0, of which waited for: 3 -> 0; matrix products, arithmetic and copies ran while one was open for 8% -> 0% of each run, Pallas kernels for 0% -> 0%
where the time goes in v1:
time: 72 us; the launch traced here: 71.3 us
  Pallas kernels  53 us (74%)
  local copies, waits for them, and re-layouts  15.2 us (21%)
  between operations  3.09 us (4%)
    pallas_call x1, Pallas kernels, local(): pl.pallas_call(functools.partial(kernel, tiles, trainers), out_shape=(lik...  53 us
    unnamed x28, local copies, waits for them, and re-layouts  15.2 us

profile of v1, /device:TPU:0, one launch (start us, length us, event | category | flops | bytes accessed | tf_op | source)
XLA Modules:
  0.0 71.3 jit_solution(14445547955590088420)
XLA Ops:
  0.6 0.0 copy-start.8
  1.3 0.7 %copy.23.routes = s32[16,1]{1,0:T(8,128)S(1)} copy(s32[16,1]{0,1:T(1,128)} %param.25) | data formatting | bytes 128 | tf_op args[12]
  2.0 0.0 copy-done.8
  2.0 0.0 copy-start
  2.0 1.0 %copy-done = f32[512,256]{1,0:T(8,128)S(1)} copy-done((f32[512,256]{1,0:T(8,128)S(1)}, f32[512,256]{1,0:T(8,128)}, u32[]{:S(2)}) %copy-start) | copy-done | bytes 524312
  3.1 0.0 copy-start.1
  3.1 1.0 %copy-done.1 = f32[512,256]{1,0:T(8,128)S(1)} copy-done((f32[512,256]{1,0:T(8,128)S(1)}, f32[512,256]{1,0:T(8,128)}, u32[]{:S(2)}) %copy-start.1) | copy-done | bytes 524312
  4.1 0.0 copy-start.2
  4.1 1.0 %copy-done.2 = f32[512,256]{1,0:T(8,128)S(1)} copy-done((f32[512,256]{1,0:T(8,128)S(1)}, f32[512,256]{1,0:T(8,128)}, u32[]{:S(2)}) %copy-start.2) | copy-done | bytes 524312
  5.2 0.9 %copy-done.3 = bf16[1024,128]{1,0:T(8,128)(2,1)S(1)} copy-done((bf16[1024,128]{1,0:T(8,128)(2,1)S(1)}, bf16[1024,128]{1,0:T(8,128)(2,1)}, u32[]{:S(2)}) %copy-start.3) | copy-done | bytes 262168
  6.1 0.9 %copy-done.4 = bf16[1024,128]{1,0:T(8,128)(2,1)S(1)} copy-done((bf16[1024,128]{1,0:T(8,128)(2,1)S(1)}, bf16[1024,128]{1,0:T(8,128)(2,1)}, u32[]{:S(2)}) %copy-start.4) | copy-done | bytes 262168
  7.1 0.9 %copy-done.5 = f32[256,128]{1,0:T(8,128)S(1)} copy-done((f32[256,128]{1,0:T(8,128)S(1)}, f32[256,128]{1,0:T(8,128)}, u32[]{:S(2)}) %copy-start.5) | copy-done | bytes 131096
  8.0 0.9 %copy-done.6 = f32[256,128]{1,0:T(8,128)S(1)} copy-done((f32[256,128]{1,0:T(8,128)S(1)}, f32[256,128]{1,0:T(8,128)}, u32[]{:S(2)}) %copy-start.6) | copy-done | bytes 131096
  8.9 0.9 %copy-done.7 = f32[256,128]{1,0:T(8,128)S(1)} copy-done((f32[256,128]{1,0:T(8,128)S(1)}, f32[256,128]{1,0:T(8,128)}, u32[]{:S(2)}) %copy-start.7) | copy-done | bytes 131096
  9.8 53.0 %shard_map.204 = (bf16[1024,128]{1,0:T(8,128)(2,1)S(1)}, f32[1,1]{1,0:T(1,128)}, bf16[512,1024]{1,0:T(8,128)(2,1)S(1)}, bf16[1024,128]{1,0:T(8,128)(2,1)S(1)}, f...) custom-call(bf16[1024,512]{1,0:T(8,128)(2,1)} %columns.1, ...), custom_call_target="tpu_custom_call" | custom-call | tf_op jit(solution)/shard_map/pallas_call | solution.py:299
  62.8 0.7 copy.35
  64.2 1.0 %copy.37 = bf16[512,1024]{1,0:T(8,128)(2,1)} copy(bf16[512,1024]{1,0:T(8,128)(2,1)S(1)} %get-tuple-element.42) | data formatting | bytes 2097152
  65.1 0.7 copy.38
  65.8 0.8 %copy.39 = f32[512,256]{1,0:T(8,128)} copy(f32[512,256]{1,0:T(8,128)S(1)} %get-tuple-element.44) | data formatting | bytes 1048576
  66.6 0.7 copy.40
  67.3 0.8 %copy.41 = f32[512,256]{1,0:T(8,128)} copy(f32[512,256]{1,0:T(8,128)S(1)} %get-tuple-element.46) | data formatting | bytes 1048576
  68.1 0.7 copy.42
  68.7 0.8 %copy.43 = f32[512,256]{1,0:T(8,128)} copy(f32[512,256]{1,0:T(8,128)S(1)} %get-tuple-element.48) | data formatting | bytes 1048576
  69.5 0.7 copy.44
  (5 shorter events, 0.0 us)
Async XLA Ops:
  0.6 1.4 %copy-start.8 = (s32[16,128]{1,0:T(8,128)S(1)}, s32[16,128]{1,0:T(8,128)}, u32[]{:S(2)}) copy-start(s32[16,128]{1,0:T(8,128)} %sampled.1) | copy-start | bytes 24580
  2.0 1.0 %copy-start = (f32[512,256]{1,0:T(8,128)S(1)}, f32[512,256]{1,0:T(8,128)}, u32[]{:S(2)}) copy-start(f32[512,256]{1,0:T(8,128)} %master_in.1) | copy-start | bytes 1572868
  3.1 1.0 %copy-start.1 = (f32[512,256]{1,0:T(8,128)S(1)}, f32[512,256]{1,0:T(8,128)}, u32[]{:S(2)}) copy-start(f32[512,256]{1,0:T(8,128)} %moment_in.1) | copy-start | bytes 1572868
  4.1 1.0 %copy-start.2 = (f32[512,256]{1,0:T(8,128)S(1)}, f32[512,256]{1,0:T(8,128)}, u32[]{:S(2)}) copy-start(f32[512,256]{1,0:T(8,128)} %second_in.1) | copy-start | bytes 1572868
  5.2 0.9 %copy-start.3 = (bf16[1024,128]{1,0:T(8,128)(2,1)S(1)}, bf16[1024,128]{1,0:T(8,128)(2,1)}, u32[]{:S(2)}) copy-start(bf16[1024,128]{1,0:T(8,128)(2,1)} %truth.1) | copy-start | bytes 786436
  6.1 0.9 %copy-start.4 = (bf16[1024,128]{1,0:T(8,128)(2,1)S(1)}, bf16[1024,128]{1,0:T(8,128)(2,1)}, u32[]{:S(2)}) copy-start(bf16[1024,128]{1,0:T(8,128)(2,1)} %weight_out.1) | copy-start | bytes 786436
  7.1 0.9 %copy-start.5 = (f32[256,128]{1,0:T(8,128)S(1)}, f32[256,128]{1,0:T(8,128)}, u32[]{:S(2)}) copy-start(f32[256,128]{1,0:T(8,128)} %master_out.1) | copy-start | bytes 393220
  8.0 0.9 %copy-start.6 = (f32[256,128]{1,0:T(8,128)S(1)}, f32[256,128]{1,0:T(8,128)}, u32[]{:S(2)}) copy-start(f32[256,128]{1,0:T(8,128)} %moment_out.1) | copy-start | bytes 393220
  8.9 0.9 %copy-start.7 = (f32[256,128]{1,0:T(8,128)S(1)}, f32[256,128]{1,0:T(8,128)}, u32[]{:S(2)}) copy-start(f32[256,128]{1,0:T(8,128)} %second_out.1) | copy-start | bytes 393220

commit v2 on v1

v2 whole, which is shorter than its diff:
```python
import functools
import jax
import jax.numpy as jnp
from jax import lax
from jax.experimental import pallas as pl
from jax.experimental.pallas import tpu as pltpu
from jax.sharding import PartitionSpec as P

BLK = 128
LANES = 128
STREAMS = 2
CHUNK = 256

rate = 0.001
first_fix = 1.0 - 0.9**8
second_fix = 1.0 - 0.999**8
f32, bf16 = jnp.float32, jnp.bfloat16


def adam_update(master, moment, second, grad):
    moment = 0.9 * moment + 0.1 * grad
    second = 0.999 * second + 0.001 * grad * grad
    master = master - rate * (moment / first_fix) / (jnp.sqrt(second / second_fix) + 1e-08)
    return (master, moment, second)


def bits_of(size):
    return size.bit_length() - 1


def stream_orders(trainers):
    ascending = list(range(bits_of(trainers)))
    return [ascending, ascending[:1] + ascending[:0:-1]]


def kernel(
    tiles, trainers,
    columns_hbm, truth_hbm, weight_in_hbm, weight_out_hbm,
    master_in, master_out, moment_in, moment_out, second_in, second_out,
    sampled_hbm, counts, routes,
    predicted_hbm, trainer_loss, fresh_in_hbm, fresh_out_hbm,
    new_master_in, new_master_out, new_moment_in, new_moment_out, new_second_in, new_second_out,
    columns, truth, weight_in, weight_out, sampled, master, moment, second,
    predicted, fresh_in, fresh_out,
    marks, pre_grads, hiddens, backs, loss_rows,
    total, outgoing, arrived_train, arrived_tile, gathered, fresh, loss_out, loss_in,
    send_sem, recv_sem, load_sem, store_sem,
):
    t, u = lax.axis_index("tile"), lax.axis_index("train")
    train_bits = bits_of(trainers)
    orders = stream_orders(trainers)
    piece = total.shape[3]
    share_rows = STREAMS * trainers * piece
    feat, width = master_in.shape
    height = master_out.shape[0]
    blocks_in = width // LANES

    def load(source, target):
        copy = pltpu.make_async_copy(source, target, load_sem.at[len(loads)])
        copy.start()
        loads.append(copy)

    def store(source, target):
        copy = pltpu.make_async_copy(source, target, store_sem.at[len(stores)])
        copy.start()
        stores.append(copy)

    loads, stores = [], []
    load(sampled_hbm, sampled)
    load(columns_hbm, columns)
    load(weight_in_hbm, weight_in)
    load(weight_out_hbm, weight_out)
    load(truth_hbm, truth)
    first_loads = len(loads)
    end_in = blocks_in * feat
    for inner, outer, flat in (
        (master_in, master_out, master), (moment_in, moment_out, moment), (second_in, second_out, second)
    ):
        for c in range(blocks_in):
            load(inner.at[:, pl.ds(c * LANES, LANES)], flat.at[pl.ds(c * feat, feat)])
        load(outer, flat.at[pl.ds(end_in, height)])
        if end_in + height < share_rows:
            missing = share_rows - end_in - height
            flat[end_in + height :, :] = jnp.zeros((missing, LANES), f32)

    def bit_of(bit):
        return (u // 2**bit) % 2

    def partner(bit):
        return {"train": u + 2**bit * (1 - 2 * bit_of(bit))}

    def other_tile(distance):
        return {"tile": (t + distance) % tiles}

    friends = [partner(bit) for bit in range(train_bits)]
    friends += [other_tile(distance) for distance in range(1, tiles)]
    barrier = pltpu.get_barrier_semaphore()
    for friend in friends:
        pl.semaphore_signal(
            barrier, inc=1, device_id=friend, device_id_type=pl.DeviceIdType.MESH
        )

    slots = sampled.shape[0]
    lane = lax.broadcasted_iota(jnp.int32, (BLK, LANES), 1)
    for b in range(slots):
        named = (lane >= trainers) | (lane == routes[0, b])
        named = named & (counts[0] > b)
        marks[b * BLK : (b + 1) * BLK, :] = jnp.where(named, 1.0, 0.0).astype(bf16)
    for copy in loads[:first_loads]:
        copy.wait()
    loss_rows[...] = jnp.zeros_like(loss_rows)

    def chunk(step, carry):
        start = pl.multiple_of(step * CHUNK, CHUNK)
        rows = pl.ds(start, CHUNK)
        own = lax.broadcasted_iota(jnp.int32, (CHUNK, LANES), 0) + start
        hits = jnp.concatenate(
            [jnp.where(own == sampled[b : b + 1, :], 1.0, 0.0).astype(bf16) for b in range(slots)],
            axis=1,
        )
        times = jnp.dot(hits, marks[...], preferred_element_type=f32)
        pre = jnp.dot(columns[rows, :], weight_in[...], preferred_element_type=f32)
        sig = 0.5 + 0.5 * jnp.tanh(0.5 * pre)
        value = pre * sig
        hidden = value.astype(bf16)
        hiddens[rows, :] = hidden
        output = jnp.dot(hidden, weight_out[...], preferred_element_type=f32)
        predicted[rows, :] = output.astype(bf16)
        error = output - truth[rows, :].astype(f32)
        squares = jnp.sum(error * error, axis=1, keepdims=True)
        loss_rows[...] += jnp.sum((squares * times).reshape(CHUNK // 8, 8, LANES), axis=0)
        often = times[:, LANES - 1 :]
        backs[rows, :] = (often * error).astype(bf16)
        hidden_grad = lax.dot_general(
            error.astype(bf16), weight_out[...], (((1,), (1,)), ((), ())),
            preferred_element_type=f32,
        )
        pre_grads[rows, :] = (often * hidden_grad * (sig + value * (1.0 - sig))).astype(bf16)
        return carry

    lax.fori_loop(0, columns.shape[0] // CHUNK, chunk, 0)
    store(predicted, predicted_hbm)

    for tile in range(tiles):
        across = slice(tile * width, (tile + 1) * width)
        part_in = lax.dot_general(
            columns[...], pre_grads[:, across], (((0,), (0,)), ((), ())),
            preferred_element_type=f32,
        )
        part_out = lax.dot_general(
            hiddens[:, tile * height : (tile + 1) * height], backs[...], (((0,), (0,)), ((), ())),
            preferred_element_type=f32,
        )
        parts = [part_in[:, c * LANES : (c + 1) * LANES] for c in range(blocks_in)] + [part_out]
        missing = share_rows - blocks_in * feat - height
        if missing:
            parts.append(jnp.zeros((missing, LANES), f32))
        total[:, :, tile] = jnp.concatenate(parts, axis=0).reshape(
            STREAMS, trainers, piece, LANES
        )

    pl.semaphore_wait(barrier, len(friends))

    used = [0]
    pending = []

    def send(source, target, friend):
        number = used[0]
        used[0] += 1
        copy = pltpu.make_async_remote_copy(
            src_ref=source,
            dst_ref=target,
            send_sem=send_sem.at[number],
            recv_sem=recv_sem.at[number],
            device_id=friend,
            device_id_type=pl.DeviceIdType.MESH,
        )
        copy.start()
        pending.append(copy)
        return copy

    starts = [0] * STREAMS
    flying = [None] * STREAMS
    losses = loss_rows[...]
    loss_copy = None
    for step in range(train_bits):
        half = 2 ** (train_bits - 1 - step)
        if loss_copy is not None:
            loss_copy.wait_recv()
            losses = losses + loss_in[step - 1]
        loss_out[step] = losses
        loss_copy = send(loss_out.at[step], loss_in.at[step], partner(step))
        for s in range(STREAMS):
            if step:
                flying[s].wait_recv()
                total[s, pl.ds(starts[s], 2 * half)] += arrived_train[s, 2 * half : 4 * half].astype(f32)
            bit = orders[s][step]
            mine = bit_of(bit)
            away = pl.ds(starts[s] + (1 - mine) * half, half)
            outgoing[s, away] = total[s, away].astype(bf16)
            flying[s] = send(
                outgoing.at[s, away], arrived_train.at[s, pl.ds(half, half)], partner(bit)
            )
            starts[s] = starts[s] + mine * half
    tile_copies = [[] for _ in range(STREAMS)]
    for s in range(STREAMS):
        flying[s].wait_recv()
        total[s, starts[s]] += arrived_train[s, 1].astype(f32)
        for distance in range(1, tiles):
            away = (t + distance) % tiles
            outgoing[s, starts[s], away] = total[s, starts[s], away].astype(bf16)
            tile_copies[s].append(
                send(
                    outgoing.at[s, starts[s], away],
                    arrived_tile.at[s, distance],
                    other_tile(distance),
                )
            )
    loss_copy.wait_recv()
    losses = losses + loss_in[train_bits - 1]
    mine_only = lax.broadcasted_iota(jnp.int32, losses.shape, 1) == u
    trainer_loss[...] = jnp.sum(
        jnp.where(mine_only, losses, 0.0), axis=(0, 1), keepdims=True
    ) / (BLK * weight_out.shape[1])

    for copy in loads[first_loads:]:
        copy.wait()
    scale = 2.0 / BLK
    grad_copies = [None] * STREAMS
    grad_begin, begin = list(starts), list(starts)

    def pass_grads(s, step):
        size = 2 ** (train_bits - 1 - step)
        if step < train_bits - 1:
            grad_copies[s].wait_recv()
            grad_begin[s] = grad_begin[s] - bit_of(orders[s][step + 1]) * (size // 2)
        region = gathered.at[s, pl.ds(grad_begin[s], size)]
        grad_copies[s] = send(region, region, partner(orders[s][step]))

    def pass_fresh(s, step):
        size = 2 ** (train_bits - 1 - step)
        if step < train_bits - 1:
            flying[s].wait_recv()
            begin[s] = begin[s] - bit_of(orders[s][step + 1]) * (size // 2)
        region = fresh.at[s, pl.ds(begin[s], size)]
        flying[s] = send(region, region, partner(orders[s][step]))

    for s in range(STREAMS):
        done = total[s, starts[s], t]
        for distance in range(1, tiles):
            tile_copies[s][distance - 1].wait_recv()
            done = done + arrived_tile[s, distance].astype(f32)
        rounded = done.astype(bf16)
        gathered[s, starts[s]] = rounded
        rows = pl.ds(pl.multiple_of((s * trainers + starts[s]) * piece, piece), piece)
        updated, _, _ = adam_update(
            master[rows, :], moment[rows, :], second[rows, :], scale * rounded.astype(f32)
        )
        fresh[s, starts[s], t] = updated.astype(bf16)
        own = fresh.at[s, starts[s], t]
        tile_copies[s] = [send(own, own, other_tile(distance)) for distance in range(1, tiles)]
        pass_grads(s, train_bits - 1)
    for step in reversed(range(1, train_bits - 1)):
        for s in range(STREAMS):
            pass_grads(s, step)
    for s in range(STREAMS):
        for copy in tile_copies[s]:
            copy.wait_recv()
        pass_fresh(s, train_bits - 1)
    for s in range(STREAMS):
        pass_grads(s, 0)
    for s in range(STREAMS):
        grad_copies[s].wait_recv()
    for s in range(STREAMS):
        for q in range(trainers):
            first = (s * trainers + q) * piece
            rows = slice(first, first + piece)
            changed = adam_update(
                master[rows, :], moment[rows, :], second[rows, :],
                scale * gathered[s, q].astype(f32),
            )
            master[rows, :], moment[rows, :], second[rows, :] = changed
    for inner, outer, flat in (
        (new_master_in, new_master_out, master),
        (new_moment_in, new_moment_out, moment),
        (new_second_in, new_second_out, second),
    ):
        for c in range(blocks_in):
            store(flat.at[pl.ds(c * feat, feat)], inner.at[:, pl.ds(c * LANES, LANES)])
        store(flat.at[pl.ds(end_in, height)], outer)
    for step in reversed(range(train_bits - 1)):
        for s in range(STREAMS):
            pass_fresh(s, step)
    for s in range(STREAMS):
        flying[s].wait_recv()
    for tile in range(tiles):
        flat = fresh[:, :, tile].reshape(share_rows, LANES)
        for c in range(blocks_in):
            left = tile * width + c * LANES
            fresh_in[:, left : left + LANES] = flat[c * feat : (c + 1) * feat]
        fresh_out[tile * height : (tile + 1) * height, :] = flat[end_in : end_in + height]
    store(fresh_in, fresh_in_hbm)
    store(fresh_out, fresh_out_hbm)
    for copy in pending:
        copy.wait_send()
    for copy in stores:
        copy.wait()


def store_kernel(*refs):
    count = (len(refs) - 1) // 2
    sources, targets, sem = refs[:count], refs[count:-1], refs[-1]
    copies = []
    for number in range(count):
        if number != 1:
            copy = pltpu.make_async_copy(sources[number], targets[number], sem.at[number])
            copy.start()
            copies.append(copy)
    targets[1][...] = sources[1][...]
    for copy in copies:
        copy.wait()


def local(
    columns, truth, weight_in, weight_out,
    master_in, master_out, moment_in, moment_out, second_in, second_out,
    counts, sampled, routes,
):
    tiles, trainers = lax.axis_size("tile"), lax.axis_size("train")
    train_bits = bits_of(trainers)
    rows, feat = columns.shape
    hidden, outs = weight_out.shape
    slots = sampled.shape[0]
    needed = (feat * master_in.shape[1] + master_out.shape[0] * outs) // LANES
    piece = -(-needed // (STREAMS * trainers * 16)) * 16
    copies = STREAMS * (3 * train_bits + 2 * (tiles - 1)) + train_bits
    blocks_in = master_in.shape[1] // LANES
    flat = (STREAMS * trainers * piece, LANES)
    vmem, hbm = pl.BlockSpec(memory_space=pltpu.VMEM), pl.BlockSpec(memory_space=pltpu.HBM)
    smem = pl.BlockSpec(memory_space=pltpu.SMEM)
    like = lambda a: jax.ShapeDtypeStruct(a.shape, a.dtype)
    results = pl.pallas_call(
        functools.partial(kernel, tiles, trainers),
        out_shape=(
            like(truth),
            jax.ShapeDtypeStruct((1, 1), f32),
            like(weight_in),
            like(weight_out),
            like(master_in), like(master_out),
            like(moment_in), like(moment_out),
            like(second_in), like(second_out),
        ),
        in_specs=[hbm] * 11 + [smem] * 2,
        out_specs=(hbm, vmem) + (hbm,) * 8,
        scratch_shapes=[
            pltpu.VMEM(columns.shape, bf16),
            pltpu.VMEM(truth.shape, bf16),
            pltpu.VMEM(weight_in.shape, bf16),
            pltpu.VMEM(weight_out.shape, bf16),
            pltpu.VMEM(sampled.shape, jnp.int32),
            pltpu.VMEM(flat, f32),
            pltpu.VMEM(flat, f32),
            pltpu.VMEM(flat, f32),
            pltpu.VMEM(truth.shape, bf16),
            pltpu.VMEM(weight_in.shape, bf16),
            pltpu.VMEM(weight_out.shape, bf16),
            pltpu.VMEM((slots * BLK, LANES), bf16),
            pltpu.VMEM((rows, hidden), bf16),
            pltpu.VMEM((rows, hidden), bf16),
            pltpu.VMEM((rows, outs), bf16),
            pltpu.VMEM((8, LANES), f32),
            pltpu.VMEM((STREAMS, trainers, tiles, piece, LANES), f32),
            pltpu.VMEM((STREAMS, trainers, tiles, piece, LANES), bf16),
            pltpu.VMEM((STREAMS, trainers, tiles, piece, LANES), bf16),
            pltpu.VMEM((STREAMS, tiles, piece, LANES), bf16),
            pltpu.VMEM((STREAMS, trainers, piece, LANES), bf16),
            pltpu.VMEM((STREAMS, trainers, tiles, piece, LANES), bf16),
            pltpu.VMEM((train_bits, 8, LANES), f32),
            pltpu.VMEM((train_bits, 8, LANES), f32),
            pltpu.SemaphoreType.DMA((copies,)),
            pltpu.SemaphoreType.DMA((copies,)),
            pltpu.SemaphoreType.DMA((5 + 3 * (blocks_in + 1),)),
            pltpu.SemaphoreType.DMA((3 + 3 * (blocks_in + 1),)),
        ],
        compiler_params=pltpu.CompilerParams(
            collective_id=0, has_side_effects=True, vmem_limit_bytes=59 * 2**20
        ),
    )(
        columns, truth, weight_in, weight_out,
        master_in, master_out, moment_in, moment_out, second_in, second_out,
        sampled, counts, routes.reshape(1, slots),
    )
    stored = pl.pallas_call(
        store_kernel,
        out_shape=(
            like(truth),
            jax.ShapeDtypeStruct((1, 1), f32),
            like(weight_in), like(weight_out),
            like(master_in), like(master_out),
            like(moment_in), like(moment_out),
            like(second_in), like(second_out),
        ),
        in_specs=[hbm, vmem] + [hbm] * 8,
        out_specs=(hbm, vmem) + (hbm,) * 8,
        scratch_shapes=[pltpu.SemaphoreType.DMA((10,))],
        compiler_params=pltpu.CompilerParams(vmem_limit_bytes=59 * 2**20),
    )(*results)
    return (stored[0], stored[1].reshape(1)) + tuple(stored[2:])


def solution(mesh):
    return jax.shard_map(
        local,
        mesh=mesh,
        in_specs=(
            P(("tile", "train"), None),
            P(("tile", "train"), None),
            P(),
            P(),
            P(None, "tile"),
            P("tile", None),
            P(None, "tile"),
            P("tile", None),
            P(None, "tile"),
            P("tile", None),
            P(("tile", "train")),
            P(("tile", "train"), None),
            P(("tile", "train"), None),
        ),
        out_specs=(
            P(("tile", "train"), None),
            P(("tile", "train")),
            P(),
            P(),
            P(None, "tile"),
            P("tile", None),
            P(None, "tile"),
            P("tile", None),
            P(None, "tile"),
            P("tile", None),
        ),
        check_vma=False,
    )
```

time: 72 us -> 156 us (2.17)
  Pallas kernels: 53 us -> 154 us
  local copies, waits for them, and re-layouts: 15.2 us -> 0 us
  between operations: 3.09 us -> 1.3 us
    pallas_call x0 -> x1, Pallas kernels: none -> 109 us  [local(): pl.pallas_call(store_kernel, out_shape=(like(truth), jax.ShapeDtypeStruct...]
    unnamed x28 -> x0, local copies, waits for them, and re-layouts: 15.2 us -> none
    pallas_call x1, Pallas kernels: 53 us -> 44.9 us  [local(): pl.pallas_call(functools.partial(kernel, tiles, trainers), out_shape=(lik...]
where the time goes in v2:
time: 156 us
  Pallas kernels  154 us (99%)
    pallas_call x1, Pallas kernels, local(): pl.pallas_call(store_kernel, out_shape=(like(truth), jax.ShapeDtypeStruct...  109 us
    pallas_call x1, Pallas kernels, local(): pl.pallas_call(functools.partial(kernel, tiles, trainers), out_shape=(lik...  44.9 us

profile of v2, /device:TPU:0, one launch (start us, length us, event | category | flops | bytes accessed | tf_op | source)
XLA Modules:
  0.0 155.7 jit_solution(16776612845785159977)
XLA Ops:
  1.3 44.9 %shard_map.204 = (bf16[1024,128]{1,0:T(8,128)(2,1)}, f32[1,1]{1,0:T(1,128)}, bf16[512,1024]{1,0:T(8,128)(2,1)}, bf16[1024,128]{1,0:T(8,128)(2,1)}, f32[512,256]{...) custom-call(bf16[1024,512]{1,0:T(8,128)(2,1)} %columns_hbm.1, ...), custom_call_target="tpu_custom_call" | custom-call | tf_op jit(solution)/shard_map/pallas_call | solution.py:342
  46.2 109.5 %shard_map.205 = (bf16[1024,128]{1,0:T(8,128)(2,1)}, f32[1,1]{1,0:T(1,128)}, bf16[512,1024]{1,0:T(8,128)(2,1)}, bf16[1024,128]{1,0:T(8,128)(2,1)}, f32[512,256]{...) custom-call(bf16[1024,128]{1,0:T(8,128)(2,1)} %get-tuple-element.30., ...), custom_call_target="tpu_custom_call" | custom-call | tf_op jit(solution)/shard_map/pallas_call | solution.py:393

commit v3 on v2

--- a/solution.py
+++ b/solution.py
@@ -308,16 +308,23 @@
 
 
 def store_kernel(*refs):
-    count = (len(refs) - 1) // 2
-    sources, targets, sem = refs[:count], refs[count:-1], refs[-1]
-    copies = []
-    for number in range(count):
-        if number != 1:
-            copy = pltpu.make_async_copy(sources[number], targets[number], sem.at[number])
-            copy.start()
-            copies.append(copy)
+    count = (len(refs) - 2) // 3
+    sources, targets, held = refs[:count], refs[count : 2 * count], refs[2 * count : 3 * count]
+    load_sem, store_sem = refs[-2:]
+    moved = [number for number in range(count) if number != 1]
+    loads = [
+        pltpu.make_async_copy(sources[number], held[number], load_sem.at[number]) for number in moved
+    ]
+    stores = [
+        pltpu.make_async_copy(held[number], targets[number], store_sem.at[number]) for number in moved
+    ]
+    for copy in loads:
+        copy.start()
     targets[1][...] = sources[1][...]
-    for copy in copies:
+    for first, second in zip(loads, stores):
+        first.wait()
+        second.start()
+    for copy in stores:
         copy.wait()
 
 
@@ -402,7 +409,8 @@
         ),
         in_specs=[hbm, vmem] + [hbm] * 8,
         out_specs=(hbm, vmem) + (hbm,) * 8,
-        scratch_shapes=[pltpu.SemaphoreType.DMA((10,))],
+        scratch_shapes=[pltpu.VMEM(a.shape, a.dtype) for a in results]
+        + [pltpu.SemaphoreType.DMA((len(results),))] * 2,
         compiler_params=pltpu.CompilerParams(vmem_limit_bytes=59 * 2**20),
     )(*results)
     return (stored[0], stored[1].reshape(1)) + tuple(stored[2:])

time: 156 us -> 50.7 us (0.33)
  Pallas kernels: 154 us -> 49.2 us
    pallas_call x1, Pallas kernels: 109 us -> 4.24 us  [local(): pl.pallas_call(store_kernel, out_shape=(like(truth), jax.ShapeDtypeStruct...]
where the time goes in v3:
time: 50.7 us; the launch traced here: 50.5 us
  Pallas kernels  49.2 us (97%)
  between operations  1.3 us (3%)
    pallas_call x1, Pallas kernels, local(): pl.pallas_call(functools.partial(kernel, tiles, trainers), out_shape=(lik...  44.9 us
    pallas_call x1, Pallas kernels, local(): pl.pallas_call(store_kernel, out_shape=(like(truth), jax.ShapeDtypeStruct...  4.24 us

profile of v3, /device:TPU:0, one launch (start us, length us, event | category | flops | bytes accessed | tf_op | source)
XLA Modules:
  0.0 50.5 jit_solution(12996706516481680056)
XLA Ops:
  1.3 44.9 %shard_map.204 = (bf16[1024,128]{1,0:T(8,128)(2,1)}, f32[1,1]{1,0:T(1,128)}, bf16[512,1024]{1,0:T(8,128)(2,1)}, bf16[1024,128]{1,0:T(8,128)(2,1)}, f32[512,256]{...) custom-call(bf16[1024,512]{1,0:T(8,128)(2,1)} %columns_hbm.1, ...), custom_call_target="tpu_custom_call" | custom-call | tf_op jit(solution)/shard_map/pallas_call | solution.py:349
  46.2 4.2 %shard_map.205 = (bf16[1024,128]{1,0:T(8,128)(2,1)}, f32[1,1]{1,0:T(1,128)}, bf16[512,1024]{1,0:T(8,128)(2,1)}, bf16[1024,128]{1,0:T(8,128)(2,1)}, f32[512,256]{...) custom-call(bf16[1024,128]{1,0:T(8,128)(2,1)} %get-tuple-element.30., ...), custom_call_target="tpu_custom_call" | custom-call | tf_op jit(solution)/shard_map/pallas_call | solution.py:400
